TPU v7x, 256 devices: a whole 4x4x8 slice. The times are simulated.
256 devices in a mesh: layer: 16 (over z, core), tensor: 16 (over y, x).
Axes of the slice: x: 4, y: 4, z: 8, core: 2. Of those that a mesh axis runs over, the one named last changes fastest.
Arguments:
- layer_input: bfloat16 [2, 128, 4096], P(None, None, 'tensor'), may hold values from -6 to 6
- weight: bfloat16 [16, 4096, 4096], P('layer', None, 'tensor'), may hold values from -0.09375 to 0.09375
- gain: bfloat16 [16, 4096], P('layer'), may hold values from 0.099609375 to 1.8984375
- block_mask: int32 [16, 32, 32], P('layer', None, 'tensor'), may hold values 0 or 1
Outputs:
- kept_grad: float32 [16, 4096, 4096], P('layer', None, 'tensor')
- recon_loss: float32 [16], P('layer')
Inputs may be any that keep to these rules, and one draw needn't show every extreme that they name: `block_mask`: 1 keeps a 128 x 128 block of weights, 0 prunes it.
All inputs are finite; a program needn't handle non-finite values.
Results may differ from a plain program's by a relative error of at most 0.029.
Values may be sent and summed in bfloat16 or wider, within the bound.
No kernel may reach another device: no remote copies, remote signals or barrier semaphores. Data moves between devices by JAX's collectives and lax.ppermute only.
A program may use at most 64 MiB of HBM per device.

v0:
```python
import jax
import jax.numpy as jnp
from jax import lax
from jax.sharding import PartitionSpec as P

BLOCK = 128


epsilon = 1e-05


def from_behind(value, axis, steps):
    count = lax.axis_size(axis)
    leading, last = (max(0, -steps), min(count, count - steps))
    return lax.ppermute(value, axis, [(source, source + steps) for source in range(leading, last)])


def shards(layer_input, weight, gain, block_mask):
    section_count = lax.axis_size("layer")
    section_index = lax.axis_index("layer")
    micro_count, micro_rows, col_width = layer_input.shape
    weights = weight[0]
    full_width = weights.shape[0]
    keep_mask = jnp.repeat(jnp.repeat(block_mask[0], BLOCK, axis=0), BLOCK, axis=1).astype(
        jnp.bfloat16
    )
    masked = weights * keep_mask
    gain_row = gain[0].astype(jnp.float32)
    pieces = 1
    piece_rows = micro_rows // pieces
    piece_count = micro_count * pieces
    step_count = piece_count + section_count - 1

    def layer_work(operands):
        own_rows, gathered, grad_sum, loss_sum = operands
        values = gathered.astype(jnp.float32)
        inv_rms = lax.rsqrt(jnp.mean(values * values, axis=-1, keepdims=True) + epsilon)
        normed = (values * inv_rms * gain_row).astype(jnp.bfloat16)
        teacher = jnp.dot(normed, weights, preferred_element_type=jnp.float32)
        student = jnp.dot(normed, masked, preferred_element_type=jnp.float32)
        error_rows = student - teacher
        error_bf = error_rows.astype(jnp.bfloat16)
        grad_term = lax.dot_general(
            normed, error_bf, (((0,), (0,)), ((), ())), preferred_element_type=jnp.float32
        )
        grad_sum = grad_sum + grad_term / micro_rows
        loss_sum = loss_sum + jnp.sum(error_rows * error_rows) / (micro_rows * full_width)
        outgoing = (own_rows.astype(jnp.float32) + teacher).astype(jnp.bfloat16)
        return (outgoing, grad_sum, loss_sum)

    def skip_work(operands):
        own_rows, gathered, grad_sum, loss_sum = operands
        return (jnp.zeros_like(own_rows), grad_sum, loss_sum)

    def one_step(step_index, state_tuple):
        incoming, grad_sum, loss_sum = state_tuple
        piece_index = step_index - section_index
        is_live = (piece_index >= 0) & (piece_index < piece_count)
        first_piece = lax.dynamic_index_in_dim(
            layer_input, jnp.clip(step_index, 0, piece_count - 1), 0, keepdims=False
        )
        own_rows = jnp.where(section_index == 0, first_piece, incoming)
        gathered = lax.all_gather(own_rows, "tensor", axis=1, tiled=True)
        outgoing, grad_sum, loss_sum = lax.cond(
            is_live, layer_work, skip_work, (own_rows, gathered, grad_sum, loss_sum)
        )
        incoming = from_behind(outgoing, "layer", 1)
        return (incoming, grad_sum, loss_sum)

    start_state = (
        jnp.zeros((piece_rows, col_width), jnp.bfloat16),
        jnp.zeros((full_width, col_width), jnp.float32),
        jnp.zeros((), jnp.float32),
    )
    incoming, grad_sum, loss_sum = lax.fori_loop(0, step_count, one_step, start_state)
    total_loss = lax.psum(loss_sum, "tensor")
    kept_grad = (grad_sum * keep_mask.astype(jnp.float32))[None]
    return (kept_grad, total_loss.reshape(1))


def solution(mesh):
    in_specs = (
        P(None, None, "tensor"),
        P("layer", None, "tensor"),
        P("layer", None),
        P("layer", None, "tensor"),
    )
    out_specs = (P("layer", None, "tensor"), P("layer"))
    return jax.shard_map(shards, mesh=mesh, in_specs=in_specs, out_specs=out_specs, check_vma=False)
```

profile of v0, /device:TPU:224, one launch (start us, length us, event | category | flops | bytes accessed | tf_op | source)
XLA Modules:
  0.0 1179.4 jit_solution(118354863346640473)
XLA Ops:
  8.9 11.6 broadcast_in_dim.16
  24.4 1104.6 %while.18 = (s32[]{:T(128)}, bf16[128,256]{1,0:T(8,128)(2,1)S(1)}, f32[4096,256]{1,0:T(8,128)}, f32[]{:T(128)}, s32[]{:T(128)}, /*index=5*/pred[]{:T(512)}, bf16...) while((s32[]{:T(128)}, bf16[128,256]{1,0:T(8,128)(2,1)S(1)}, ...), condition=%wide.region_5.6_spmd, body=%wide.region_0.5_spmd.sunk | while | flops 815530112 | bytes 33738180 | solution.py:75
  25.2 51.3 %all-gather.2.cloned.1.call-done = bf16[128,4096]{1,0:T(8,128)(2,1)} async-done(((bf16[128,256]{1,0:T(8,128)(2,1)}), bf16[128,4096]{1,0:T(8,128)(2,1)}) %all-gather.2.cloned.1.call-update) | async-done | bytes 1048592 | tf_op jit(solution)/shard_map/while/body/eval_jaxpr/all_gather | solution.py:63
  82.8 53.0 %all-gather.2.cloned.1.call-done = bf16[128,4096]{1,0:T(8,128)(2,1)} async-done(((bf16[128,256]{1,0:T(8,128)(2,1)}), bf16[128,4096]{1,0:T(8,128)(2,1)}) %all-gather.2.cloned.1.call-update) | async-done | bytes 1048592 | tf_op jit(solution)/shard_map/while/body/eval_jaxpr/all_gather | solution.py:63
  142.1 53.9 %all-gather.2.cloned.1.call-done = bf16[128,4096]{1,0:T(8,128)(2,1)} async-done(((bf16[128,256]{1,0:T(8,128)(2,1)}), bf16[128,4096]{1,0:T(8,128)(2,1)}) %all-gather.2.cloned.1.call-update) | async-done | bytes 1048592 | tf_op jit(solution)/shard_map/while/body/eval_jaxpr/all_gather | solution.py:63
  202.2 57.1 %all-gather.2.cloned.1.call-done = bf16[128,4096]{1,0:T(8,128)(2,1)} async-done(((bf16[128,256]{1,0:T(8,128)(2,1)}), bf16[128,4096]{1,0:T(8,128)(2,1)}) %all-gather.2.cloned.1.call-update) | async-done | bytes 1048592 | tf_op jit(solution)/shard_map/while/body/eval_jaxpr/all_gather | solution.py:63
  265.6 57.1 %all-gather.2.cloned.1.call-done = bf16[128,4096]{1,0:T(8,128)(2,1)} async-done(((bf16[128,256]{1,0:T(8,128)(2,1)}), bf16[128,4096]{1,0:T(8,128)(2,1)}) %all-gather.2.cloned.1.call-update) | async-done | bytes 1048592 | tf_op jit(solution)/shard_map/while/body/eval_jaxpr/all_gather | solution.py:63
  328.9 58.1 %all-gather.2.cloned.1.call-done = bf16[128,4096]{1,0:T(8,128)(2,1)} async-done(((bf16[128,256]{1,0:T(8,128)(2,1)}), bf16[128,4096]{1,0:T(8,128)(2,1)}) %all-gather.2.cloned.1.call-update) | async-done | bytes 1048592 | tf_op jit(solution)/shard_map/while/body/eval_jaxpr/all_gather | solution.py:63
  393.4 58.3 %all-gather.2.cloned.1.call-done = bf16[128,4096]{1,0:T(8,128)(2,1)} async-done(((bf16[128,256]{1,0:T(8,128)(2,1)}), bf16[128,4096]{1,0:T(8,128)(2,1)}) %all-gather.2.cloned.1.call-update) | async-done | bytes 1048592 | tf_op jit(solution)/shard_map/while/body/eval_jaxpr/all_gather | solution.py:63
  458.0 59.3 %all-gather.2.cloned.1.call-done = bf16[128,4096]{1,0:T(8,128)(2,1)} async-done(((bf16[128,256]{1,0:T(8,128)(2,1)}), bf16[128,4096]{1,0:T(8,128)(2,1)}) %all-gather.2.cloned.1.call-update) | async-done | bytes 1048592 | tf_op jit(solution)/shard_map/while/body/eval_jaxpr/all_gather | solution.py:63
  523.6 59.3 %all-gather.2.cloned.1.call-done = bf16[128,4096]{1,0:T(8,128)(2,1)} async-done(((bf16[128,256]{1,0:T(8,128)(2,1)}), bf16[128,4096]{1,0:T(8,128)(2,1)}) %all-gather.2.cloned.1.call-update) | async-done | bytes 1048592 | tf_op jit(solution)/shard_map/while/body/eval_jaxpr/all_gather | solution.py:63
  589.2 62.5 %all-gather.2.cloned.1.call-done = bf16[128,4096]{1,0:T(8,128)(2,1)} async-done(((bf16[128,256]{1,0:T(8,128)(2,1)}), bf16[128,4096]{1,0:T(8,128)(2,1)}) %all-gather.2.cloned.1.call-update) | async-done | bytes 1048592 | tf_op jit(solution)/shard_map/while/body/eval_jaxpr/all_gather | solution.py:63
  658.0 62.7 %all-gather.2.cloned.1.call-done = bf16[128,4096]{1,0:T(8,128)(2,1)} async-done(((bf16[128,256]{1,0:T(8,128)(2,1)}), bf16[128,4096]{1,0:T(8,128)(2,1)}) %all-gather.2.cloned.1.call-update) | async-done | bytes 1048592 | tf_op jit(solution)/shard_map/while/body/eval_jaxpr/all_gather | solution.py:63
  727.0 60.5 %all-gather.2.cloned.1.call-done = bf16[128,4096]{1,0:T(8,128)(2,1)} async-done(((bf16[128,256]{1,0:T(8,128)(2,1)}), bf16[128,4096]{1,0:T(8,128)(2,1)}) %all-gather.2.cloned.1.call-update) | async-done | bytes 1048592 | tf_op jit(solution)/shard_map/while/body/eval_jaxpr/all_gather | solution.py:63
  793.8 60.7 %all-gather.2.cloned.1.call-done = bf16[128,4096]{1,0:T(8,128)(2,1)} async-done(((bf16[128,256]{1,0:T(8,128)(2,1)}), bf16[128,4096]{1,0:T(8,128)(2,1)}) %all-gather.2.cloned.1.call-update) | async-done | bytes 1048592 | tf_op jit(solution)/shard_map/while/body/eval_jaxpr/all_gather | solution.py:63
  860.8 59.7 %all-gather.2.cloned.1.call-done = bf16[128,4096]{1,0:T(8,128)(2,1)} async-done(((bf16[128,256]{1,0:T(8,128)(2,1)}), bf16[128,4096]{1,0:T(8,128)(2,1)}) %all-gather.2.cloned.1.call-update) | async-done | bytes 1048592 | tf_op jit(solution)/shard_map/while/body/eval_jaxpr/all_gather | solution.py:63
  922.3 12.6 %collective-permute-done = bf16[128,256]{1,0:T(8,128)(2,1)S(1)} collective-permute-done((bf16[128,256]{1,0:T(8,128)(2,1)S(1)}, bf16[128,256]{1,0:T(8,128)(2,1)S(1)}, u32[]{:S(2)}, u32[]{:S(2)}) %collective-permute-start) | collective-permute-done | bytes 65568 | tf_op jit(solution)/shard_map/while/body/eval_jaxpr/ppermute | solution.py:15
  935.6 50.8 %all-gather.2.cloned.1.call-done = bf16[128,4096]{1,0:T(8,128)(2,1)} async-done(((bf16[128,256]{1,0:T(8,128)(2,1)}), bf16[128,4096]{1,0:T(8,128)(2,1)}) %all-gather.2.cloned.1.call-update) | async-done | bytes 1048592 | tf_op jit(solution)/shard_map/while/body/eval_jaxpr/all_gather | solution.py:63
  986.3 11.2 conditional.2
  1003.8 47.7 %all-gather.2.cloned.1.call-done = bf16[128,4096]{1,0:T(8,128)(2,1)} async-done(((bf16[128,256]{1,0:T(8,128)(2,1)}), bf16[128,4096]{1,0:T(8,128)(2,1)}) %all-gather.2.cloned.1.call-update) | async-done | bytes 1048592 | tf_op jit(solution)/shard_map/while/body/eval_jaxpr/all_gather | solution.py:63
  1051.4 11.2 conditional.2
  1068.9 47.7 %all-gather.2.cloned.1.call-done = bf16[128,4096]{1,0:T(8,128)(2,1)} async-done(((bf16[128,256]{1,0:T(8,128)(2,1)}), bf16[128,4096]{1,0:T(8,128)(2,1)}) %all-gather.2.cloned.1.call-update) | async-done | bytes 1048592 | tf_op jit(solution)/shard_map/while/body/eval_jaxpr/all_gather | solution.py:63
  1116.6 11.6 collective-permute-start
  1129.0 39.3 %psum.7 = f32[1]{0:T(128)} all-reduce(f32[1]{0:T(128)} %bitcast.6), channel_id=1, replica_groups=mesh['layer'=16,'tensor'=16] {'tensor'}, use_global_device_ids=true, to_apply=%region_6.7 | all-reduce | flops 1 | bytes 8 | tf_op jit(solution)/shard_map/psum | solution.py:76
  (143 shorter events, 129.3 us)
Async XLA Ops:
  24.4 52.0 %all-gather.2.cloned.1.call-start = ((), (), s32[]{:S(2)}) async-start(), calls=%async_computation | async-start | bytes 1114112 | tf_op jit(solution)/shard_map/while/body/eval_jaxpr/all_gather | solution.py:63
  82.1 53.7 %all-gather.2.cloned.1.call-start = ((), (), s32[]{:S(2)}) async-start(), calls=%async_computation | async-start | bytes 1114112 | tf_op jit(solution)/shard_map/while/body/eval_jaxpr/all_gather | solution.py:63
  141.4 54.6 %all-gather.2.cloned.1.call-start = ((), (), s32[]{:S(2)}) async-start(), calls=%async_computation | async-start | bytes 1114112 | tf_op jit(solution)/shard_map/while/body/eval_jaxpr/all_gather | solution.py:63
  196.0 5.6 collective-permute-start
  201.6 57.8 %all-gather.2.cloned.1.call-start = ((), (), s32[]{:S(2)}) async-start(), calls=%async_computation | async-start | bytes 1114112 | tf_op jit(solution)/shard_map/while/body/eval_jaxpr/all_gather | solution.py:63
  259.3 5.6 collective-permute-start
  264.9 57.8 %all-gather.2.cloned.1.call-start = ((), (), s32[]{:S(2)}) async-start(), calls=%async_computation | async-start | bytes 1114112 | tf_op jit(solution)/shard_map/while/body/eval_jaxpr/all_gather | solution.py:63
  328.3 58.8 %all-gather.2.cloned.1.call-start = ((), (), s32[]{:S(2)}) async-start(), calls=%async_computation | async-start | bytes 1114112 | tf_op jit(solution)/shard_map/while/body/eval_jaxpr/all_gather | solution.py:63
  392.6 59.1 %all-gather.2.cloned.1.call-start = ((), (), s32[]{:S(2)}) async-start(), calls=%async_computation | async-start | bytes 1114112 | tf_op jit(solution)/shard_map/while/body/eval_jaxpr/all_gather | solution.py:63
  457.3 60.1 %all-gather.2.cloned.1.call-start = ((), (), s32[]{:S(2)}) async-start(), calls=%async_computation | async-start | bytes 1114112 | tf_op jit(solution)/shard_map/while/body/eval_jaxpr/all_gather | solution.py:63
  517.3 5.6 collective-permute-start
  522.9 60.1 %all-gather.2.cloned.1.call-start = ((), (), s32[]{:S(2)}) async-start(), calls=%async_computation | async-start | bytes 1114112 | tf_op jit(solution)/shard_map/while/body/eval_jaxpr/all_gather | solution.py:63
  583.0 5.6 collective-permute-start
  588.5 63.2 %all-gather.2.cloned.1.call-start = ((), (), s32[]{:S(2)}) async-start(), calls=%async_computation | async-start | bytes 1114112 | tf_op jit(solution)/shard_map/while/body/eval_jaxpr/all_gather | solution.py:63
  657.3 63.5 %all-gather.2.cloned.1.call-start = ((), (), s32[]{:S(2)}) async-start(), calls=%async_computation | async-start | bytes 1114112 | tf_op jit(solution)/shard_map/while/body/eval_jaxpr/all_gather | solution.py:63
  726.3 61.1 %all-gather.2.cloned.1.call-start = ((), (), s32[]{:S(2)}) async-start(), calls=%async_computation | async-start | bytes 1114112 | tf_op jit(solution)/shard_map/while/body/eval_jaxpr/all_gather | solution.py:63
  787.5 5.6 collective-permute-start
  793.1 61.5 %all-gather.2.cloned.1.call-start = ((), (), s32[]{:S(2)}) async-start(), calls=%async_computation | async-start | bytes 1114112 | tf_op jit(solution)/shard_map/while/body/eval_jaxpr/all_gather | solution.py:63
  860.1 60.3 %all-gather.2.cloned.1.call-start = ((), (), s32[]{:S(2)}) async-start(), calls=%async_computation | async-start | bytes 1114112 | tf_op jit(solution)/shard_map/while/body/eval_jaxpr/all_gather | solution.py:63
  920.4 14.5 %collective-permute-start = (bf16[128,256]{1,0:T(8,128)(2,1)S(1)}, bf16[128,256]{1,0:T(8,128)(2,1)S(1)}, u32[]{:S(2)}, u32[]{:S(2)}) collective-permute-start(bf16[128,256]{1,0:T(8,128)(2,1)S(1)} %get-tuple-element.326), channel_id=1, source_target_pairs={{0,16},{16,32},{32,48},{48,64},{64,80},{80,96},{96,112},{112,128},... | collective-permute-start | bytes 196616 | tf_op jit(solution)/shard_map/while/body/eval_jaxpr/ppermute | solution.py:15
  934.9 51.4 %all-gather.2.cloned.1.call-start = ((), (), s32[]{:S(2)}) async-start(), calls=%async_computation | async-start | bytes 1114112 | tf_op jit(solution)/shard_map/while/body/eval_jaxpr/all_gather | solution.py:63
  1003.1 48.3 %all-gather.2.cloned.1.call-start = ((), (), s32[]{:S(2)}) async-start(), calls=%async_computation | async-start | bytes 1114112 | tf_op jit(solution)/shard_map/while/body/eval_jaxpr/all_gather | solution.py:63
  1068.2 48.3 %all-gather.2.cloned.1.call-start = ((), (), s32[]{:S(2)}) async-start(), calls=%async_computation | async-start | bytes 1114112 | tf_op jit(solution)/shard_map/while/body/eval_jaxpr/all_gather | solution.py:63
  1116.6 12.5 %collective-permute-start = (bf16[128,256]{1,0:T(8,128)(2,1)S(1)}, bf16[128,256]{1,0:T(8,128)(2,1)S(1)}, u32[]{:S(2)}, u32[]{:S(2)}) collective-permute-start(bf16[128,256]{1,0:T(8,128)(2,1)S(1)} %get-tuple-element.326), channel_id=1, source_target_pairs={{0,16},{16,32},{32,48},{48,64},{64,80},{80,96},{96,112},{112,128},... | collective-permute-start | bytes 196616 | tf_op jit(solution)/shard_map/while/body/eval_jaxpr/ppermute | solution.py:15
  (16 other events, 80.7 us)
Sparse Core Ops, SparseCore 0:
  27.7 48.7 all-gather.1
  85.3 50.4 all-gather.1
  144.6 51.3 all-gather.1
  204.5 54.8 all-gather.1
  267.8 54.8 all-gather.1
  331.2 55.7 all-gather.1
  395.8 55.7 all-gather.1
  460.5 56.7 all-gather.1
  526.1 56.7 all-gather.1
  591.5 60.1 all-gather.1
  660.5 60.1 all-gather.1
  729.2 58.1 all-gather.1
  796.3 58.1 all-gather.1
  863.0 57.3 all-gather.1
  937.8 48.4 all-gather.1
  1006.0 45.3 all-gather.1
  1071.1 45.3 all-gather.1
where the time goes:
time: 1180 us
  waiting for transfers between devices  1030 us (87%)
  starting transfers between devices  42.2 us (4%)
  blocking collectives  39.3 us (3%)
  other arithmetic  21.3 us (2%)
  matrix products  17.3 us (1%)
  local copies, waits for them, and re-layouts  15 us (1%)
  between operations  13.7 us (1%)
    all_gather x17, waiting for transfers between devices, one_step(): gathered = lax.all_gather(own_rows, 'tensor', axis=1, tiled=True)  960 us
    ppermute x17, waiting for transfers between devices, from_behind(): lax.ppermute(value, axis, [(source, source + steps) for source in range(l...  68.2 us
    ppermute x17, starting transfers between devices, from_behind(): lax.ppermute(value, axis, [(source, source + steps) for source in range(l...  42.1 us
    psum x1, blocking collectives, shards(): total_loss = lax.psum(loss_sum, 'tensor')  39.3 us
  transfers between devices with their start and end apart: 34, of which 34 were waited for; matrix products, arithmetic and copies ran while one was open for 0% of the time, Pallas kernels for 0%

commit v1 on v0

v1 whole, which is shorter than its diff:
```python
import jax
import jax.numpy as jnp
from jax import lax
from jax.experimental import pallas as pl
from jax.experimental.pallas import tpu as pltpu
from jax.sharding import PartitionSpec as P

BLOCK = 128
EPSILON = 1e-05
AXES = ("layer", "tensor")


def vmem():
    return pl.BlockSpec(memory_space=pltpu.VMEM)


def smem():
    return pl.BlockSpec(memory_space=pltpu.SMEM)


def hbm():
    return pl.BlockSpec(memory_space=pl.ANY)


def chain_kernel(place, own, blocks, gain, weights, kept_in, out, kept, sem):
    count, rows, width = blocks.shape
    save = pltpu.make_async_copy(blocks, kept.at[place[1]], sem)

    @pl.when(place[0] == 1)
    def _():
        save.start()

    squares = jnp.zeros((rows, width), jnp.float32)
    total = jnp.zeros((rows, weights.shape[1]), jnp.float32)
    for s in range(count):
        x = blocks[s].astype(jnp.float32)
        squares = squares + x * x
        scaled = (x * gain[s : s + 1, :].astype(jnp.float32)).astype(jnp.bfloat16)
        total = total + jnp.dot(
            scaled, weights[s * width : (s + 1) * width, :], preferred_element_type=jnp.float32
        )
    mean = jnp.sum(squares, axis=1, keepdims=True) / (count * width)
    new = (own[...].astype(jnp.float32) + lax.rsqrt(mean + EPSILON) * total).astype(jnp.bfloat16)
    for s in range(out.shape[0]):
        out[s] = new

    @pl.when(place[0] == 1)
    def _():
        save.wait()


def chain_layer(place, own, blocks, gain, weights, kept):
    return pl.pallas_call(
        chain_kernel,
        out_shape=(
            jax.ShapeDtypeStruct(blocks.shape, jnp.bfloat16),
            jax.ShapeDtypeStruct(kept.shape, kept.dtype),
        ),
        in_specs=[smem(), vmem(), vmem(), vmem(), vmem(), hbm()],
        out_specs=(vmem(), hbm()),
        scratch_shapes=[pltpu.SemaphoreType.DMA],
        input_output_aliases={5: 1},
        compiler_params=pltpu.CompilerParams(vmem_limit_bytes=32 * 1024 * 1024),
        name="chain_layer",
    )(place, own, blocks, gain, weights, kept)


def save_kernel(place, blocks, kept_in, kept, sem):
    @pl.when(place[0] == 1)
    def _():
        save = pltpu.make_async_copy(blocks, kept.at[place[1]], sem)
        save.start()
        save.wait()


def save_rows(place, blocks, kept):
    return pl.pallas_call(
        save_kernel,
        out_shape=jax.ShapeDtypeStruct(kept.shape, kept.dtype),
        in_specs=[smem(), hbm(), hbm()],
        out_specs=hbm(),
        scratch_shapes=[pltpu.SemaphoreType.DMA],
        input_output_aliases={2: 0},
        name="save_rows",
    )(place, blocks, kept)


def error_kernel(first, second, gain, weights, keep, normed, error_bf, loss):
    count, rows, width = first.shape
    for half, source in enumerate((first, second)):
        span = slice(half * rows, (half + 1) * rows)
        squares = jnp.zeros((rows, width), jnp.float32)
        for s in range(count):
            x = source[s].astype(jnp.float32)
            squares = squares + x * x
        inv = lax.rsqrt(jnp.sum(squares, axis=1, keepdims=True) / (count * width) + EPSILON)
        for s in range(count):
            x = source[s].astype(jnp.float32)
            normed[s, span, :] = (x * inv * gain[s : s + 1, :].astype(jnp.float32)).astype(jnp.bfloat16)
    total = jnp.zeros((2 * rows, weights.shape[1]), jnp.float32)
    per = width // BLOCK
    for s in range(count):
        for b in range(per):
            i = s * per + b
            pruned = weights[i * BLOCK : (i + 1) * BLOCK, :] * (1 - keep[i : i + 1, :]).astype(jnp.bfloat16)
            total = total - jnp.dot(
                normed[s, :, b * BLOCK : (b + 1) * BLOCK], pruned, preferred_element_type=jnp.float32
            )
    error_bf[...] = total.astype(jnp.bfloat16)
    part = jnp.sum(total * total, axis=0, keepdims=True)
    part = part[:, :128] + part[:, 128:]
    loss[...] = jnp.broadcast_to(part, loss.shape)


def grad_kernel(normed, error_bf, keep, out):
    width = normed.shape[2]
    product = lax.dot_general(
        normed[0], error_bf[...], (((0,), (0,)), ((), ())), preferred_element_type=jnp.float32
    )
    for b in range(width // BLOCK):
        span = slice(b * BLOCK, (b + 1) * BLOCK)
        out[span, :] = product[span, :] * (1.0 / 128) * keep[0, b : b + 1, :]


def tail(first, second, gain, weights, keep, full_width, micro_rows):
    count, rows, width = first.shape
    cols = weights.shape[1]
    normed, error_bf, loss = pl.pallas_call(
        error_kernel,
        out_shape=(
            jax.ShapeDtypeStruct((count, 2 * rows, width), jnp.bfloat16),
            jax.ShapeDtypeStruct((2 * rows, cols), jnp.bfloat16),
            jax.ShapeDtypeStruct((8, 128), jnp.float32),
        ),
        in_specs=[vmem()] * 5,
        out_specs=(vmem(),) * 3,
        compiler_params=pltpu.CompilerParams(vmem_limit_bytes=32 * 1024 * 1024),
        name="layer_error",
    )(first, second, gain, weights, keep)
    grad = pl.pallas_call(
        grad_kernel,
        grid=(count,),
        out_shape=jax.ShapeDtypeStruct((count * width, cols), jnp.float32),
        in_specs=[
            pl.BlockSpec((1, 2 * rows, width), lambda s: (s, 0, 0)),
            pl.BlockSpec((2 * rows, cols), lambda s: (0, 0)),
            pl.BlockSpec((1, width // BLOCK, cols), lambda s: (s, 0, 0)),
        ],
        out_specs=pl.BlockSpec((width, cols), lambda s: (s, 0)),
        compiler_params=pltpu.CompilerParams(vmem_limit_bytes=32 * 1024 * 1024),
        name="layer_grad",
    )(normed, error_bf, keep.reshape(count, width // BLOCK, cols))
    shares = lax.all_to_all(jnp.broadcast_to(loss, (16, 8, 128)), "tensor", 0, 0)
    total = jnp.sum(shares[:, 0, :]) / (micro_rows * full_width)
    return grad, total


def shards(layer_input, weight, gain, block_mask):
    layers = lax.axis_size("layer")
    tensors = lax.axis_size("tensor")
    planes = layers // 2
    layer = lax.axis_index("layer")
    plane, core = layer // 2, layer % 2
    micro, rows, width = layer_input.shape
    weights = weight[0]
    full_width = weights.shape[0]
    everyone = [(l, t) for l in range(layers) for t in range(tensors)]
    swap = [(l * tensors + t, (l ^ 1) * tensors + t) for l, t in everyone]
    hop = [(l * tensors + t, ((l + 2) % layers) * tensors + t) for l, t in everyone]

    gains = gain[0].reshape(tensors, width)
    other_weights = lax.ppermute(weights, AXES, swap)
    other_gains = lax.ppermute(gains, AXES, swap)
    first = core == 0
    w = (jnp.where(first, weights, other_weights), jnp.where(first, other_weights, weights))
    g = (jnp.where(first, gains, other_gains), jnp.where(first, other_gains, gains))

    kept = jnp.zeros((2, tensors, rows, width), jnp.bfloat16)
    own = lax.dynamic_index_in_dim(layer_input, core, 0, keepdims=False)
    send = jnp.broadcast_to(own, (tensors, rows, width))
    for step in range(planes):
        for parity in (0, 1):
            place = jnp.stack(
                [(plane == step).astype(jnp.int32), (core != parity).astype(jnp.int32)]
            )
            if step and not parity:
                own = lax.ppermute(own, AXES, hop)
                send = jnp.broadcast_to(own, (tensors, rows, width))
            blocks = lax.all_to_all(send, "tensor", 0, 0)
            if step == planes - 1 and parity:
                kept = save_rows(place, blocks, kept)
            else:
                send, kept = chain_layer(place, own, blocks, g[parity], w[parity], kept)
                own = send[0]
    arrived = lax.ppermute(kept[1], AXES, swap)
    keep = jnp.repeat(block_mask[0].astype(jnp.float32), BLOCK, axis=1)
    grad, total = tail(kept[0], arrived, gains, weights, keep, full_width, rows)
    return grad[None], total.reshape(1)


def solution(mesh):
    in_specs = (
        P(None, None, "tensor"),
        P("layer", None, "tensor"),
        P("layer", None),
        P("layer", None, "tensor"),
    )
    out_specs = (P("layer", None, "tensor"), P("layer"))
    return jax.shard_map(shards, mesh=mesh, in_specs=in_specs, out_specs=out_specs, check_vma=False)
```

time: 1180 us -> 457 us (0.39)
  waiting for transfers between devices: 1030 us -> 243 us
  Pallas kernels: 0 us -> 61 us
  starting transfers between devices: 42.2 us -> 86.1 us
  local copies, waits for them, and re-layouts: 15 us -> 54.4 us
  blocking collectives: 39.3 us -> 0 us
  matrix products: 17.3 us -> 0 us
  other arithmetic: 21.3 us -> 6.31 us
    all_gather x17 -> x0, waiting for transfers between devices: 960 us -> none  [one_step(): gathered = lax.all_gather(own_rows, 'tensor', axis=1, tiled=True)]
    all_to_all x0 -> x17, waiting for transfers between devices: none -> 223 us  [the longest x16 223 us: shards(): blocks = lax.all_to_all(send, 'tensor', 0, 0)]
    all_to_all x0 -> x17, starting transfers between devices: none -> 65.7 us  [the longest x16 62.2 us: shards(): blocks = lax.all_to_all(send, 'tensor', 0, 0)]
    pallas_call x0 -> x18, Pallas kernels: none -> 61 us  [the longest x1 33.5 us: save_rows(): pl.pallas_call(save_kernel, out_shape=jax.ShapeDtypeStruct(kept.shape, ke...]
    ppermute x17 -> x10, waiting for transfers between devices: 68.2 us -> 20.3 us  [the longest x7 16.4 us: shards(): own = lax.ppermute(own, AXES, hop)]
    psum x1 -> x0, blocking collectives: 39.3 us -> none  [shards(): total_loss = lax.psum(loss_sum, 'tensor')]
    unnamed x4 -> x65, local copies, waits for them, and re-layouts: 0.01 us -> 35.9 us
    ppermute x17 -> x10, starting transfers between devices: 42.1 us -> 20.4 us  [the longest x7 20.2 us: shards(): own = lax.ppermute(own, AXES, hop)]
  transfers between devices with their start and end apart: 34 -> 27, of which waited for: 34 -> 25; matrix products, arithmetic and copies ran while one was open for 0% -> 3% of each run, Pallas kernels for 0% -> 2%
where the time goes in v1:
time: 457 us; the launch traced here: 454 us
  waiting for transfers between devices  243 us (53%)
  starting transfers between devices  86.1 us (19%)
  Pallas kernels  61 us (13%)
  local copies, waits for them, and re-layouts  54.4 us (12%)
  other arithmetic  6.31 us (1%)
    all_to_all x16, waiting for transfers between devices, shards(): blocks = lax.all_to_all(send, 'tensor', 0, 0)  223 us
    all_to_all x16, starting transfers between devices, shards(): blocks = lax.all_to_all(send, 'tensor', 0, 0)  62.2 us
    unnamed x65, local copies, waits for them, and re-layouts  35.9 us
    pallas_call x1, Pallas kernels, save_rows(): pl.pallas_call(save_kernel, out_shape=jax.ShapeDtypeStruct(kept.shape, ke...  33.5 us
    ppermute x7, starting transfers between devices, shards(): own = lax.ppermute(own, AXES, hop)  20.2 us
    pallas_call x15, Pallas kernels, chain_layer(): pl.pallas_call(chain_kernel, out_shape=(jax.ShapeDtypeStruct(blocks.shape...  16.9 us
    ppermute x7, waiting for transfers between devices, shards(): own = lax.ppermute(own, AXES, hop)  16.4 us
  transfers between devices with their start and end apart: 27, of which 25 were waited for; matrix products, arithmetic and copies ran while one was open for 3% of the time, Pallas kernels for 2%

profile of v1, /device:TPU:224, one launch (start us, length us, event | category | flops | bytes accessed | tf_op | source)
XLA Modules:
  0.0 454.1 jit_solution(15413603083446315572)
XLA Ops:
  2.6 7.0 %all-to-all-start = ((bf16[16,128,256]{2,1,0:T(8,128)(2,1)}), bf16[16,128,256]{2,1,0:T(8,128)(2,1)S(1)}, u32[]{:S(2)}, u32[]{:S(2)}) async-start(bf16[16,128,256]{2,1,0:T(8,128)(2,1)} %broadcast_in_dim.36), calls=%async_computation | async-start | bytes 2097152 | tf_op jit(solution)/shard_map/all_to_all | solution.py:189
  11.0 3.9 broadcast_select_fusion
  14.9 12.4 %all-to-all-done.blocks = bf16[16,128,256]{2,1,0:T(8,128)(2,1)S(1)} async-done(((bf16[16,128,256]{2,1,0:T(8,128)(2,1)}), bf16[16,128,256]{2,1,0:T(8,128)(2,1)S(1)}, u32[]{:S(2)}, u32[]{:S(2)}) %all-to-all-start) | async-done | bytes 1048608 | tf_op jit(solution)/shard_map/all_to_all | solution.py:189
  35.6 15.4 %all-to-all-done.1.blocks = bf16[16,128,256]{2,1,0:T(8,128)(2,1)S(1)} async-done(((bf16[16,128,256]{2,1,0:T(8,128)(2,1)}), bf16[16,128,256]{2,1,0:T(8,128)(2,1)S(1)}, u32[]{:S(2)}, u32[]{:S(2)}) %all-to-all-start.1) | async-done | bytes 1048608 | tf_op jit(solution)/shard_map/all_to_all | solution.py:189
  53.8 4.3 collective-permute-done.2.own
  62.9 15.2 %all-to-all-done.2.blocks = bf16[16,128,256]{2,1,0:T(8,128)(2,1)S(1)} async-done(((bf16[16,128,256]{2,1,0:T(8,128)(2,1)}), bf16[16,128,256]{2,1,0:T(8,128)(2,1)S(1)}, u32[]{:S(2)}, u32[]{:S(2)}) %all-to-all-start.2) | async-done | bytes 1048608 | tf_op jit(solution)/shard_map/all_to_all | solution.py:189
  86.3 13.4 %all-to-all-done.3.blocks = bf16[16,128,256]{2,1,0:T(8,128)(2,1)S(1)} async-done(((bf16[16,128,256]{2,1,0:T(8,128)(2,1)}), bf16[16,128,256]{2,1,0:T(8,128)(2,1)S(1)}, u32[]{:S(2)}, u32[]{:S(2)}) %all-to-all-start.3) | async-done | bytes 1048608 | tf_op jit(solution)/shard_map/all_to_all | solution.py:189
  111.6 13.2 %all-to-all-done.4.blocks = bf16[16,128,256]{2,1,0:T(8,128)(2,1)S(1)} async-done(((bf16[16,128,256]{2,1,0:T(8,128)(2,1)}), bf16[16,128,256]{2,1,0:T(8,128)(2,1)S(1)}, u32[]{:S(2)}, u32[]{:S(2)}) %all-to-all-start.4) | async-done | bytes 1048608 | tf_op jit(solution)/shard_map/all_to_all | solution.py:189
  133.1 12.4 %all-to-all-done.5.blocks = bf16[16,128,256]{2,1,0:T(8,128)(2,1)S(1)} async-done(((bf16[16,128,256]{2,1,0:T(8,128)(2,1)}), bf16[16,128,256]{2,1,0:T(8,128)(2,1)S(1)}, u32[]{:S(2)}, u32[]{:S(2)}) %all-to-all-start.5) | async-done | bytes 1048608 | tf_op jit(solution)/shard_map/all_to_all | solution.py:189
  157.8 13.2 %all-to-all-done.6.blocks = bf16[16,128,256]{2,1,0:T(8,128)(2,1)S(1)} async-done(((bf16[16,128,256]{2,1,0:T(8,128)(2,1)}), bf16[16,128,256]{2,1,0:T(8,128)(2,1)S(1)}, u32[]{:S(2)}, u32[]{:S(2)}) %all-to-all-start.6) | async-done | bytes 1048608 | tf_op jit(solution)/shard_map/all_to_all | solution.py:189
  179.3 12.4 %all-to-all-done.7.blocks = bf16[16,128,256]{2,1,0:T(8,128)(2,1)S(1)} async-done(((bf16[16,128,256]{2,1,0:T(8,128)(2,1)}), bf16[16,128,256]{2,1,0:T(8,128)(2,1)S(1)}, u32[]{:S(2)}, u32[]{:S(2)}) %all-to-all-start.7) | async-done | bytes 1048608 | tf_op jit(solution)/shard_map/all_to_all | solution.py:189
  204.7 13.3 %all-to-all-done.8.blocks = bf16[16,128,256]{2,1,0:T(8,128)(2,1)S(1)} async-done(((bf16[16,128,256]{2,1,0:T(8,128)(2,1)}), bf16[16,128,256]{2,1,0:T(8,128)(2,1)S(1)}, u32[]{:S(2)}, u32[]{:S(2)}) %all-to-all-start.8) | async-done | bytes 1048608 | tf_op jit(solution)/shard_map/all_to_all | solution.py:189
  226.5 12.4 %all-to-all-done.9.blocks = bf16[16,128,256]{2,1,0:T(8,128)(2,1)S(1)} async-done(((bf16[16,128,256]{2,1,0:T(8,128)(2,1)}), bf16[16,128,256]{2,1,0:T(8,128)(2,1)S(1)}, u32[]{:S(2)}, u32[]{:S(2)}) %all-to-all-start.9) | async-done | bytes 1048608 | tf_op jit(solution)/shard_map/all_to_all | solution.py:189
  252.0 15.0 %all-to-all-done.10.blocks = bf16[16,128,256]{2,1,0:T(8,128)(2,1)S(1)} async-done(((bf16[16,128,256]{2,1,0:T(8,128)(2,1)}), bf16[16,128,256]{2,1,0:T(8,128)(2,1)S(1)}, u32[]{:S(2)}, u32[]{:S(2)}) %all-to-all-start.10) | async-done | bytes 1048608 | tf_op jit(solution)/shard_map/all_to_all | solution.py:189
  270.6 3.9 all-to-all-start.11
  275.4 12.5 %all-to-all-done.11.blocks = bf16[16,128,256]{2,1,0:T(8,128)(2,1)S(1)} async-done(((bf16[16,128,256]{2,1,0:T(8,128)(2,1)}), bf16[16,128,256]{2,1,0:T(8,128)(2,1)S(1)}, u32[]{:S(2)}, u32[]{:S(2)}) %all-to-all-start.11) | async-done | bytes 1048608 | tf_op jit(solution)/shard_map/all_to_all | solution.py:189
  301.1 20.4 %all-to-all-done.12.blocks = bf16[16,128,256]{2,1,0:T(8,128)(2,1)S(1)} async-done(((bf16[16,128,256]{2,1,0:T(8,128)(2,1)}), bf16[16,128,256]{2,1,0:T(8,128)(2,1)S(1)}, u32[]{:S(2)}, u32[]{:S(2)}) %all-to-all-start.12) | async-done | bytes 1048608 | tf_op jit(solution)/shard_map/all_to_all | solution.py:189
  329.7 13.7 %all-to-all-done.13.blocks = bf16[16,128,256]{2,1,0:T(8,128)(2,1)S(1)} async-done(((bf16[16,128,256]{2,1,0:T(8,128)(2,1)}), bf16[16,128,256]{2,1,0:T(8,128)(2,1)S(1)}, u32[]{:S(2)}, u32[]{:S(2)}) %all-to-all-start.13) | async-done | bytes 1048608 | tf_op jit(solution)/shard_map/all_to_all | solution.py:189
  346.1 4.5 collective-permute-start.8
  353.6 3.8 all-to-all-start.14
  357.5 15.4 %all-to-all-done.14.blocks = bf16[16,128,256]{2,1,0:T(8,128)(2,1)S(1)} async-done(((bf16[16,128,256]{2,1,0:T(8,128)(2,1)}), bf16[16,128,256]{2,1,0:T(8,128)(2,1)S(1)}, u32[]{:S(2)}, u32[]{:S(2)}) %all-to-all-start.14) | async-done | bytes 1048608 | tf_op jit(solution)/shard_map/all_to_all | solution.py:189
  381.0 12.7 %all-to-all-done.15.blocks = bf16[16,128,256]{2,1,0:T(8,128)(2,1)S(1)} async-done(((bf16[16,128,256]{2,1,0:T(8,128)(2,1)}), bf16[16,128,256]{2,1,0:T(8,128)(2,1)S(1)}, u32[]{:S(2)}, u32[]{:S(2)}) %all-to-all-start.15) | async-done | bytes 1048608 | tf_op jit(solution)/shard_map/all_to_all | solution.py:189
  394.6 33.5 %save_rows.1 = bf16[2,16,128,256]{3,2,1,0:T(8,128)(2,1)} custom-call(s32[2]{0:T(128)} %pad_add_fusion.1.place, bf16[16,128,256]{2,1,0:T(8,128)(2,1)} %copy-done.29, bf16[2,16,128,256]{3,2,1,0:T(8,128)(2,1)} %copy-done.1), custom_call_target="tpu_custom_call", output_to_operand_aliasing={{}: (2, {})} | custom-call | tf_op jit(solution)/shard_map/save_rows/pallas_call | solution.py:77
  444.0 7.7 %layer_grad.1 = f32[4096,256]{1,0:T(8,128)} custom-call(bf16[16,256,256]{2,1,0:T(8,128)(2,1)S(1)} %copy-done.20, bf16[256,256]{1,0:T(8,128)(2,1)S(1)} %get-tuple-element.66.error_bf, f32[16,2,256]{2,1,0:T(2,128)S(1)} %reshape_reshape.3.keep), custom_call_target="tpu_custom_call" | custom-call | tf_op jit(solution)/shard_map/layer_grad/pallas_call | solution.py:140
  (165 shorter events, 159.4 us)
Async XLA Ops:
  0.7 10.4 %collective-permute-start.1 = (bf16[4096,256]{1,0:T(8,128)(2,1)}, bf16[4096,256]{1,0:T(8,128)(2,1)}, u32[]{:S(2)}, u32[]{:S(2)}) collective-permute-start(bf16[4096,256]{1,0:T(8,128)(2,1)} %bitcast.56), channel_id=1, source_target_pairs={{0,16},{1,17},{2,18},{3,19},{4,20},{5,21},{6,22},{7,23},{8,24},{9,... | collective-permute-start | bytes 6291464 | tf_op jit(solution)/shard_map/ppermute | solution.py:172
  2.6 24.7 %all-to-all-start = ((bf16[16,128,256]{2,1,0:T(8,128)(2,1)}), bf16[16,128,256]{2,1,0:T(8,128)(2,1)S(1)}, u32[]{:S(2)}, u32[]{:S(2)}) async-start(bf16[16,128,256]{2,1,0:T(8,128)(2,1)} %broadcast_in_dim.36), calls=%async_computation | async-start | bytes 2097152 | tf_op jit(solution)/shard_map/all_to_all | solution.py:189
  31.0 20.0 %all-to-all-start.1 = ((bf16[16,128,256]{2,1,0:T(8,128)(2,1)}), bf16[16,128,256]{2,1,0:T(8,128)(2,1)S(1)}, u32[]{:S(2)}, u32[]{:S(2)}) async-start(bf16[16,128,256]{2,1,0:T(8,128)(2,1)} %copy-done.21), calls=%async_computation.1 | async-start | bytes 2097152 | tf_op jit(solution)/shard_map/all_to_all | solution.py:189
  53.7 4.3 collective-permute-start.2
  59.1 18.9 %all-to-all-start.2 = ((bf16[16,128,256]{2,1,0:T(8,128)(2,1)}), bf16[16,128,256]{2,1,0:T(8,128)(2,1)S(1)}, u32[]{:S(2)}, u32[]{:S(2)}) async-start(bf16[16,128,256]{2,1,0:T(8,128)(2,1)} %broadcast_in_dim.38), calls=%async_computation.2 | async-start | bytes 2097152 | tf_op jit(solution)/shard_map/all_to_all | solution.py:189
  81.7 18.0 %all-to-all-start.3 = ((bf16[16,128,256]{2,1,0:T(8,128)(2,1)}), bf16[16,128,256]{2,1,0:T(8,128)(2,1)S(1)}, u32[]{:S(2)}, u32[]{:S(2)}) async-start(bf16[16,128,256]{2,1,0:T(8,128)(2,1)} %copy-done.22), calls=%async_computation.3 | async-start | bytes 2097152 | tf_op jit(solution)/shard_map/all_to_all | solution.py:189
  107.9 17.0 %all-to-all-start.4 = ((bf16[16,128,256]{2,1,0:T(8,128)(2,1)}), bf16[16,128,256]{2,1,0:T(8,128)(2,1)S(1)}, u32[]{:S(2)}, u32[]{:S(2)}) async-start(bf16[16,128,256]{2,1,0:T(8,128)(2,1)} %broadcast_in_dim.39), calls=%async_computation.4 | async-start | bytes 2097152 | tf_op jit(solution)/shard_map/all_to_all | solution.py:189
  128.5 17.0 %all-to-all-start.5 = ((bf16[16,128,256]{2,1,0:T(8,128)(2,1)}), bf16[16,128,256]{2,1,0:T(8,128)(2,1)S(1)}, u32[]{:S(2)}, u32[]{:S(2)}) async-start(bf16[16,128,256]{2,1,0:T(8,128)(2,1)} %copy-done.23), calls=%async_computation.5 | async-start | bytes 2097152 | tf_op jit(solution)/shard_map/all_to_all | solution.py:189
  148.2 4.8 %collective-permute-start.4 = (bf16[128,256]{1,0:T(8,128)(2,1)S(1)}, bf16[128,256]{1,0:T(8,128)(2,1)S(1)}, u32[]{:S(2)}, u32[]{:S(2)}) collective-permute-start(bf16[128,256]{1,0:T(8,128)(2,1)S(1)} %slice_bitcast_fusion.10), channel_id=1, source_target_pairs={{0,32},{1,33},{2,34},{3,35},{4,36},{5,37},{6,38},{7,39},{8,40},{9,... | collective-permute-start | bytes 196616 | tf_op jit(solution)/shard_map/ppermute | solution.py:187
  154.1 17.0 %all-to-all-start.6 = ((bf16[16,128,256]{2,1,0:T(8,128)(2,1)}), bf16[16,128,256]{2,1,0:T(8,128)(2,1)S(1)}, u32[]{:S(2)}, u32[]{:S(2)}) async-start(bf16[16,128,256]{2,1,0:T(8,128)(2,1)} %broadcast_in_dim.40), calls=%async_computation.6 | async-start | bytes 2097152 | tf_op jit(solution)/shard_map/all_to_all | solution.py:189
  174.7 17.0 %all-to-all-start.7 = ((bf16[16,128,256]{2,1,0:T(8,128)(2,1)}), bf16[16,128,256]{2,1,0:T(8,128)(2,1)S(1)}, u32[]{:S(2)}, u32[]{:S(2)}) async-start(bf16[16,128,256]{2,1,0:T(8,128)(2,1)} %copy-done.24), calls=%async_computation.7 | async-start | bytes 2097152 | tf_op jit(solution)/shard_map/all_to_all | solution.py:189
  194.4 5.6 %collective-permute-start.5 = (bf16[128,256]{1,0:T(8,128)(2,1)S(1)}, bf16[128,256]{1,0:T(8,128)(2,1)S(1)}, u32[]{:S(2)}, u32[]{:S(2)}) collective-permute-start(bf16[128,256]{1,0:T(8,128)(2,1)S(1)} %slice_bitcast_fusion.8), channel_id=1, source_target_pairs={{0,32},{1,33},{2,34},{3,35},{4,36},{5,37},{6,38},{7,39},{8,40},{9,... | collective-permute-start | bytes 196616 | tf_op jit(solution)/shard_map/ppermute | solution.py:187
  201.0 17.1 %all-to-all-start.8 = ((bf16[16,128,256]{2,1,0:T(8,128)(2,1)}), bf16[16,128,256]{2,1,0:T(8,128)(2,1)S(1)}, u32[]{:S(2)}, u32[]{:S(2)}) async-start(bf16[16,128,256]{2,1,0:T(8,128)(2,1)} %broadcast_in_dim.41), calls=%async_computation.8 | async-start | bytes 2097152 | tf_op jit(solution)/shard_map/all_to_all | solution.py:189
  221.9 17.0 %all-to-all-start.9 = ((bf16[16,128,256]{2,1,0:T(8,128)(2,1)}), bf16[16,128,256]{2,1,0:T(8,128)(2,1)S(1)}, u32[]{:S(2)}, u32[]{:S(2)}) async-start(bf16[16,128,256]{2,1,0:T(8,128)(2,1)} %copy-done.25), calls=%async_computation.9 | async-start | bytes 2097152 | tf_op jit(solution)/shard_map/all_to_all | solution.py:189
  241.6 5.6 %collective-permute-start.6 = (bf16[128,256]{1,0:T(8,128)(2,1)S(1)}, bf16[128,256]{1,0:T(8,128)(2,1)S(1)}, u32[]{:S(2)}, u32[]{:S(2)}) collective-permute-start(bf16[128,256]{1,0:T(8,128)(2,1)S(1)} %slice_bitcast_fusion.6), channel_id=1, source_target_pairs={{0,32},{1,33},{2,34},{3,35},{4,36},{5,37},{6,38},{7,39},{8,40},{9,... | collective-permute-start | bytes 196616 | tf_op jit(solution)/shard_map/ppermute | solution.py:187
  248.2 18.7 %all-to-all-start.10 = ((bf16[16,128,256]{2,1,0:T(8,128)(2,1)}), bf16[16,128,256]{2,1,0:T(8,128)(2,1)S(1)}, u32[]{:S(2)}, u32[]{:S(2)}) async-start(bf16[16,128,256]{2,1,0:T(8,128)(2,1)} %broadcast_in_dim.42), calls=%async_computation.10 | async-start | bytes 2097152 | tf_op jit(solution)/shard_map/all_to_all | solution.py:189
  270.6 17.3 %all-to-all-start.11 = ((bf16[16,128,256]{2,1,0:T(8,128)(2,1)}), bf16[16,128,256]{2,1,0:T(8,128)(2,1)S(1)}, u32[]{:S(2)}, u32[]{:S(2)}) async-start(bf16[16,128,256]{2,1,0:T(8,128)(2,1)} %copy-done.26), calls=%async_computation.11 | async-start | bytes 2097152 | tf_op jit(solution)/shard_map/all_to_all | solution.py:189
  290.7 5.6 %collective-permute-start.7 = (bf16[128,256]{1,0:T(8,128)(2,1)S(1)}, bf16[128,256]{1,0:T(8,128)(2,1)S(1)}, u32[]{:S(2)}, u32[]{:S(2)}) collective-permute-start(bf16[128,256]{1,0:T(8,128)(2,1)S(1)} %slice_bitcast_fusion.4), channel_id=1, source_target_pairs={{0,32},{1,33},{2,34},{3,35},{4,36},{5,37},{6,38},{7,39},{8,40},{9,... | collective-permute-start | bytes 196616 | tf_op jit(solution)/shard_map/ppermute | solution.py:187
  297.3 24.1 %all-to-all-start.12 = ((bf16[16,128,256]{2,1,0:T(8,128)(2,1)}), bf16[16,128,256]{2,1,0:T(8,128)(2,1)S(1)}, u32[]{:S(2)}, u32[]{:S(2)}) async-start(bf16[16,128,256]{2,1,0:T(8,128)(2,1)} %broadcast_in_dim.43), calls=%async_computation.12 | async-start | bytes 2097152 | tf_op jit(solution)/shard_map/all_to_all | solution.py:189
  325.1 18.3 %all-to-all-start.13 = ((bf16[16,128,256]{2,1,0:T(8,128)(2,1)}), bf16[16,128,256]{2,1,0:T(8,128)(2,1)S(1)}, u32[]{:S(2)}, u32[]{:S(2)}) async-start(bf16[16,128,256]{2,1,0:T(8,128)(2,1)} %copy-done.27), calls=%async_computation.13 | async-start | bytes 2097152 | tf_op jit(solution)/shard_map/all_to_all | solution.py:189
  346.1 6.4 %collective-permute-start.8 = (bf16[128,256]{1,0:T(8,128)(2,1)S(1)}, bf16[128,256]{1,0:T(8,128)(2,1)S(1)}, u32[]{:S(2)}, u32[]{:S(2)}) collective-permute-start(bf16[128,256]{1,0:T(8,128)(2,1)S(1)} %slice_bitcast_fusion.2), channel_id=1, source_target_pairs={{0,32},{1,33},{2,34},{3,35},{4,36},{5,37},{6,38},{7,39},{8,40},{9,... | collective-permute-start | bytes 196616 | tf_op jit(solution)/shard_map/ppermute | solution.py:187
  353.6 19.4 %all-to-all-start.14 = ((bf16[16,128,256]{2,1,0:T(8,128)(2,1)}), bf16[16,128,256]{2,1,0:T(8,128)(2,1)S(1)}, u32[]{:S(2)}, u32[]{:S(2)}) async-start(bf16[16,128,256]{2,1,0:T(8,128)(2,1)} %broadcast_in_dim.44), calls=%async_computation.14 | async-start | bytes 2097152 | tf_op jit(solution)/shard_map/all_to_all | solution.py:189
  376.7 17.0 %all-to-all-start.15 = ((bf16[16,128,256]{2,1,0:T(8,128)(2,1)}), bf16[16,128,256]{2,1,0:T(8,128)(2,1)S(1)}, u32[]{:S(2)}, u32[]{:S(2)}) async-start(bf16[16,128,256]{2,1,0:T(8,128)(2,1)} %copy-done.28), calls=%async_computation.15 | async-start | bytes 2097152 | tf_op jit(solution)/shard_map/all_to_all | solution.py:189
  438.9 12.9 %all-to-all-start.16 = ((f32[16,8,128]{2,1,0:T(8,128)}), f32[16,8,128]{2,1,0:T(8,128)S(1)}, u32[]{:S(2)}, u32[]{:S(2)}) async-start(f32[16,8,128]{2,1,0:T(8,128)} %broadcast_in_dim.47), calls=%async_computation.16 | async-start | bytes 131072 | tf_op jit(solution)/shard_map/all_to_all | solution.py:153
  (35 other events, 90.1 us)
